TPU v7x, 1024 devices: a whole 8x8x8 slice. The times are simulated.
1024 devices in a mesh: replica: 16 (over y, core), fsdp: 64 (over x, z).
Axes of the slice: x: 8, y: 8, z: 8, core: 2. Of those that a mesh axis runs over, the one named last changes fastest.
Arguments:
- grad_part: bfloat16 [16, 64, 7168, 128], P('replica', None, 'fsdp'), may hold values from -6 to 6
- momentum: float32 [64, 7168, 128], P('replica', 'fsdp'), may hold values from -24 to 24
- row_counts: int32 [64], replicated, may hold values from 512 to 7168, as said below
Outputs:
- new_momentum: float32 [64, 7168, 128], P('replica', 'fsdp')
- update: bfloat16 [64, 7168, 128], P('replica', 'fsdp')
Inputs may be any that keep to these rules, and one draw needn't show every extreme that they name: `row_counts`: each matrix has 7168 rows (an output projection head) or 512 rows (a key or value head); both kinds occur.
All inputs are finite; a program needn't handle non-finite values.
Results may differ from a plain program's by a relative error of at most 0.04.
Values may be sent and summed in bfloat16 or wider, within the bound.
A program may use at most 32 MiB of HBM per device.

v0:
```python
import jax
import jax.numpy as jnp
from jax import lax
from jax.sharding import PartitionSpec as P

ITERS = 3


def newton_whole(xmat):
    for step in range(ITERS):
        gram = lax.dot_general(
            xmat, xmat, (((0,), (0,)), ((), ())), preferred_element_type=jnp.float32
        ).astype(jnp.bfloat16)
        poly = (
            -4.775 * gram.astype(jnp.float32)
            + 2.0315 * jnp.dot(gram, gram, preferred_element_type=jnp.float32)
        ).astype(jnp.bfloat16)
        xmat = (
            3.4445 * xmat.astype(jnp.float32)
            + jnp.dot(xmat, poly, preferred_element_type=jnp.float32)
        ).astype(jnp.bfloat16)
    return xmat


def per_device(grad_part, momentum, row_counts):
    summed = lax.psum_scatter(grad_part[0], "replica", scatter_dimension=0, tiled=True).astype(
        jnp.float32
    )
    group = lax.axis_index("replica")
    piece = lax.axis_index("fsdp")
    mat_count, shard_rows, head_cols = momentum.shape
    counts = lax.dynamic_slice_in_dim(row_counts, group * mat_count, mat_count)
    rows = piece * shard_rows + jnp.arange(shard_rows, dtype=jnp.int32)
    live = rows[None, :, None] < counts[:, None, None]
    new_momentum = jnp.where(live, 0.95 * momentum + summed, jnp.float32(0.0))
    rounded = new_momentum.astype(jnp.bfloat16)
    devices = lax.axis_size("fsdp")
    stride = devices // mat_count
    outgoing = jnp.repeat(rounded, stride, axis=0)
    arrived = lax.all_to_all(outgoing, "fsdp", split_axis=0, concat_axis=0, tiled=True)
    whole = arrived.reshape(devices * shard_rows, head_cols)
    wide = whole.astype(jnp.float32)
    start = (wide / (jnp.sqrt(jnp.sum(wide * wide)) + 1e-07)).astype(jnp.bfloat16)
    result = newton_whole(start)
    leader = piece % stride == 0
    sending = jnp.where(leader, result, jnp.zeros_like(result))
    returned = lax.all_to_all(
        sending.reshape(devices, shard_rows, head_cols),
        "fsdp",
        split_axis=0,
        concat_axis=0,
        tiled=True,
    )
    ortho = jnp.sum(
        returned.reshape(mat_count, stride, shard_rows, head_cols).astype(jnp.float32), axis=1
    ).astype(jnp.bfloat16)
    scale = 0.2 * jnp.sqrt(counts.astype(jnp.float32))
    update = (ortho.astype(jnp.float32) * scale[:, None, None]).astype(jnp.bfloat16)
    return (new_momentum, update)


def solution(mesh):
    in_specs = (P("replica", None, "fsdp", None), P("replica", "fsdp", None), P())
    out_specs = (P("replica", "fsdp", None), P("replica", "fsdp", None))
    return jax.shard_map(
        per_device, mesh=mesh, in_specs=in_specs, out_specs=out_specs, check_vma=False
    )
```

profile of v0, /device:TPU:118, one launch (start us, length us, event | category | flops | bytes accessed | tf_op | source)
XLA Modules:
  0.0 230.5 jit_solution(1962466893556556505)
XLA Ops:
  7.2 0.0 copy-start.3
  7.2 0.0 copy-start.2
  7.2 0.0 reduce-scatter.2.cloned.1.call-start
  7.2 0.7 reduce-scatter.2.cloned.1.call-update
  7.9 0.1 sqrt_multiply_fusion
  8.0 0.1 broadcast_compare_fusion
  8.1 73.7 %reduce-scatter.2.cloned.1.call-done = bf16[4,112,128]{2,1,0:T(8,128)(2,1)} async-done(((bf16[64,112,128]{2,1,0:T(8,128)(2,1)}), bf16[4,112,128]{2,1,0:T(8,128)(2,1)}) %reduce-scatter.2.cloned.1.call-update) | async-done | bytes 114704 | tf_op jit(solution)/shard_map/reduce_scatter | solution.py:26
  81.8 1.7 fusion.31
  83.5 1.5 broadcast_in_dim.23
  85.0 14.1 %all-to-all-start = ((bf16[64,112,128]{2,1,0:T(8,128)(2,1)}), bf16[64,112,128]{2,1,0:T(8,128)(2,1)S(1)}, u32[]{:S(2)}, u32[]{:S(2)}) async-start(bf16[64,112,128]{2,1,0:T(8,128)(2,1)} %bitcast.26), calls=%async_computation.1 | async-start | bytes 3670016 | tf_op jit(solution)/shard_map/all_to_all | solution.py:40
  99.1 50.6 %all-to-all-done = bf16[64,112,128]{2,1,0:T(8,128)(2,1)S(1)} async-done(((bf16[64,112,128]{2,1,0:T(8,128)(2,1)}), bf16[64,112,128]{2,1,0:T(8,128)(2,1)S(1)}, u32[]{:S(2)}, u32[]{:S(2)}) %all-to-all-start) | async-done | bytes 1835040 | tf_op jit(solution)/shard_map/all_to_all | solution.py:40
  149.7 1.5 fusion.4
  152.0 0.4 fusion.5
  152.3 0.0 copy-start
  152.3 0.7 fusion.9
  153.0 0.6 copy-done
  153.6 2.8 %fusion = bf16[7168,128]{1,0:T(8,128)(2,1)S(1)} fusion(bf16[7168,128]{1,0:T(8,128)(2,1)} %bitcast.25, bf16[128,128]{1,0:T(8,128)(2,1)S(1)} %fusion.9), kind=kOutput, calls=%fused_computation.3 | convolution fusion | flops 242827264 | bytes 3702784 | tf_op jit(solution)/shard_map/dot_general | solution.py:20
  156.4 0.7 convolution_convert_fusion.1
  157.1 2.0 fusion.1
  159.1 2.9 %convolution_convert_fusion = bf16[128,128]{1,0:T(8,128)(2,1)S(1)} fusion(bf16[7168,128]{1,0:T(8,128)(2,1)} %fusion.1), kind=kOutput, calls=%fused_computation.23 | convolution fusion | flops 234897408 | bytes 1867776 | tf_op jit(solution)/shard_map/dot_general | solution.py:11
  162.0 2.1 fusion.3
  164.1 58.6 %all_to_all.10 = bf16[64,112,128]{2,1,0:T(8,128)(2,1)S(1)} all-to-all(bf16[64,112,128]{2,1,0:T(8,128)(2,1)} %bitcast.28), channel_id=1, replica_groups=mesh['replica'=16,'fsdp'=64] {'fsdp'}, dimensions={0} | all-to-all | bytes 3670016 | tf_op jit(solution)/shard_map/all_to_all | solution.py:47
  222.7 0.2 bitcast_reduce_fusion
  222.9 0.7 multiply_convert_fusion
  (5 shorter events, 0.0 us)
Async XLA Ops:
  7.2 0.8 copy-start.3
  7.2 74.6 %copy-start.2 = (f32[4,112,128]{2,1,0:T(8,128)S(1)}, f32[4,112,128]{2,1,0:T(8,128)}, u32[]{:S(2)}) copy-start(f32[4,112,128]{2,1,0:T(8,128)} %param.4) | copy-start | bytes 688132
  7.2 74.6 %reduce-scatter.2.cloned.1.call-start = ((), (), s32[]{:S(2)}) async-start(), calls=%async_computation.3 | async-start | bytes 1949696 | tf_op jit(solution)/shard_map/reduce_scatter | solution.py:26
  85.0 64.7 %all-to-all-start = ((bf16[64,112,128]{2,1,0:T(8,128)(2,1)}), bf16[64,112,128]{2,1,0:T(8,128)(2,1)S(1)}, u32[]{:S(2)}, u32[]{:S(2)}) async-start(bf16[64,112,128]{2,1,0:T(8,128)(2,1)} %bitcast.26), calls=%async_computation.1 | async-start | bytes 3670016 | tf_op jit(solution)/shard_map/all_to_all | solution.py:40
  152.3 1.3 copy-start
  159.1 2.9 %copy-start.1 = (bf16[7168,128]{1,0:T(8,128)(2,1)S(1)}, bf16[7168,128]{1,0:T(8,128)(2,1)}, u32[]{:S(2)}) copy-start(bf16[7168,128]{1,0:T(8,128)(2,1)} %fusion.1) | copy-start | bytes 5505028
Sparse Core Ops, SparseCore 0:
  11.4 70.3 reduce-scatter.1
where the time goes:
time: 231 us
  waiting for transfers between devices  125 us (54%)
  blocking collectives  58.6 us (25%)
  between operations  14.8 us (6%)
  starting transfers between devices  14.1 us (6%)
  matrix products  11.2 us (5%)
  other arithmetic  4.75 us (2%)
    reduce_scatter x1, waiting for transfers between devices, per_device(): lax.psum_scatter(grad_part[0], 'replica', scatter_dimension=0, tiled=True)  73.7 us
    all_to_all x1, blocking collectives, per_device(): lax.all_to_all(sending.reshape(devices, shard_rows, head_cols), 'fsdp', s...  58.6 us
    all_to_all x1, waiting for transfers between devices, per_device(): lax.all_to_all(outgoing, 'fsdp', split_axis=0, concat_axis=0, tiled=True)  50.6 us
    all_to_all x1, starting transfers between devices, per_device(): lax.all_to_all(outgoing, 'fsdp', split_axis=0, concat_axis=0, tiled=True)  14.1 us
    dot_general x3, matrix products, newton_whole(): jnp.dot(xmat, poly, preferred_element_type=jnp.float32)  6.96 us
  transfers between devices with their start and end apart: 2, of which 2 were waited for; matrix products, arithmetic and copies ran while one was open for 0% of the time, Pallas kernels for 0%

commit v1 on v0

v1 whole, which is shorter than its diff:
```python
import functools

import jax
import jax.numpy as jnp
from jax import lax
from jax.experimental import pallas as pl
from jax.experimental.pallas import tpu as pltpu
from jax.sharding import PartitionSpec as P

ITERS = 3
MESH = pl.DeviceIdType.MESH
F32 = jnp.float32
BF16 = jnp.bfloat16
COEF = (3.4445, -4.775, 2.0315)


def ring_messages(ring, mats):
    slots = {}
    for matrix in range(mats):
        for hops in range(ring // 2, 0, -1):
            for way in (0, 1):
                if hops < ring // 2 or matrix % 2 == way:
                    slots[way, hops, matrix] = len(slots)
    return slots


def split(a):
    high = a.astype(BF16)
    return high, (a - high.astype(F32)).astype(BF16)


def product(a, b):
    a_high, a_low = split(a)
    b_high, b_low = split(b)
    return jnp.dot(
        jnp.concatenate([a_high, a_low, a_high], axis=1),
        jnp.concatenate([b_high, b_high, b_low], axis=0),
        preferred_element_type=F32,
    )


def polynomials(grams, eye):
    total = None
    for step in range(ITERS):
        squares = [product(g, g) for g in grams]
        factors = [COEF[0] * eye + COEF[1] * g + COEF[2] * s for g, s in zip(grams, squares)]
        if step < ITERS - 1:
            halves = [product(g, f) for g, f in zip(grams, factors)]
            grams = [product(h, f) for h, f in zip(halves, factors)]
        total = factors if total is None else [product(t, f) for t, f in zip(total, factors)]
    return total


def kernel(
    ring,
    side,
    slots,
    grad,
    momentum,
    row_counts,
    new_momentum,
    update,
    own,
    sib,
    stage,
    landed,
    mom,
    new_mom,
    rounded,
    result,
    counts,
    packed,
    parts1,
    chunk1,
    parts2,
    chunk2,
    full,
    load_sem,
    out_sem,
    sib_send,
    sib_recv,
    ring_send,
    ring_recv,
    sum_send,
    sum_recv,
):
    mats, rows, cols = mom.shape
    half = cols // 2
    part = chunk1.shape[1]
    replica = lax.axis_index("replica")
    fsdp = lax.axis_index("fsdp")
    y, core = replica // 2, lax.rem(replica, 2)
    x, z = fsdp // side, lax.rem(fsdp, side)
    sibling = (2 * y + 1 - core, fsdp)
    ahead = (2 * lax.rem(y + 1, ring) + core, fsdp)
    behind = (2 * lax.rem(y + ring - 1, ring) + core, fsdp)

    def along(axis, d):
        if axis == 0:
            return (replica, lax.rem(x + d, side) * side + z)
        return (replica, x * side + lax.rem(z + d, side))

    barrier = pltpu.get_barrier_semaphore()
    peers = [sibling, ahead, behind]
    peers += [along(axis, d) for axis in (0, 1) for d in range(1, side)]
    for peer in peers:
        pl.semaphore_signal(barrier, inc=1, device_id=peer, device_id_type=MESH)

    order = [ring // 2]
    for hops in range(ring // 2 - 1, 0, -1):
        order += [hops, ring - hops]
    order += [0]

    def chunk_of(o, which):
        return pl.ds((2 * lax.rem(y + o, ring) + which) * mats, mats)

    loads = {}
    for o in order:
        loads[o] = pltpu.make_async_copy(
            grad.at[0, chunk_of(o, core)], own.at[o], load_sem.at[o]
        )
        loads[o].start()
    load_mom = pltpu.make_async_copy(momentum, mom, load_sem.at[ring])
    load_mom.start()
    load_counts = pltpu.make_async_copy(row_counts, counts, load_sem.at[ring + 1])
    load_counts.start()

    pl.semaphore_wait(barrier, len(peers))

    exchange = {}
    for o in order:
        exchange[o] = pltpu.make_async_remote_copy(
            src_ref=grad.at[0, chunk_of(o, 1 - core)],
            dst_ref=sib.at[o],
            send_sem=sib_send.at[o],
            recv_sem=sib_recv.at[o],
            device_id=sibling,
            device_id_type=MESH,
        )
        exchange[o].start()

    ready = set()

    def pair_sum(o, j):
        if o not in ready:
            loads[o].wait()
            exchange[o].wait_recv()
            ready.add(o)
        return own[o, j].astype(F32) + sib[o, j].astype(F32)

    hop = {}

    def ring_step(hops, chosen):
        for j in chosen:
            for way in (0, 1):
                slot = slots.get((way, hops, j))
                if slot is None:
                    continue
                value = pair_sum(hops if way == 0 else ring - hops, j)
                before = slots.get((way, hops + 1, j))
                if before is not None:
                    hop[before].wait_recv()
                    value = value + landed[before].astype(F32)
                stage[slot] = value.astype(BF16)
                hop[slot] = pltpu.make_async_remote_copy(
                    src_ref=stage.at[slot],
                    dst_ref=landed.at[slot],
                    send_sem=ring_send.at[slot],
                    recv_sem=ring_recv.at[slot],
                    device_id=(ahead, behind)[way],
                    device_id_type=MESH,
                )
                hop[slot].start()

    outs = []
    row = fsdp * rows + lax.broadcasted_iota(jnp.int32, (rows, cols), 0)
    lane = lax.broadcasted_iota(jnp.int32, (half, cols), 1)
    left = lane < half
    eye = (
        lax.broadcasted_iota(jnp.int32, (cols, cols), 0)
        == lax.broadcasted_iota(jnp.int32, (cols, cols), 1)
    ).astype(F32)

    def finish_sum(j):
        value = pair_sum(0, j)
        for way in (0, 1):
            slot = slots[way, 1, j]
            hop[slot].wait_recv()
            value = value + landed[slot].astype(F32)
        moved = jnp.where(row < counts[replica * mats + j], 0.95 * mom[j] + value, 0.0)
        new_mom[j] = moved
        out = pltpu.make_async_copy(new_mom.at[j], new_momentum.at[j], out_sem.at[j])
        out.start()
        outs.append(out)
        r = moved.astype(BF16)
        rounded[j] = r
        return lax.dot_general(r, r, (((0,), (0,)), ((), ())), preferred_element_type=F32)

    sends = []

    def send_sum(a, phase, d, src, dst, axis):
        at = (a * 3 + phase) * (side - 1) + d - 1
        copy = pltpu.make_async_remote_copy(
            src_ref=src,
            dst_ref=dst,
            send_sem=sum_send.at[at],
            recv_sem=sum_recv.at[at],
            device_id=along(axis, d),
            device_id_type=MESH,
        )
        copy.start()
        sends.append(copy)
        return copy

    def piece(index):
        return pl.ds(pl.multiple_of(index * part, 8), part)

    flight = {}

    def place(axis):
        return x if axis == 0 else z

    def sum_scatter(a, first, second):
        packed[a, :half] = jnp.where(left, first[:half], first[half:])
        packed[a, half : 2 * half] = jnp.where(left, second[:half], second[half:])
        packed[a, 2 * half :] = jnp.where(left, first[half:], second[:half])
        flight[a] = [
            send_sum(
                a,
                0,
                d,
                packed.at[a, piece(lax.rem(place(a) + d, side))],
                parts1.at[a, d - 1],
                a,
            )
            for d in range(1, side)
        ]

    def sum_across(a):
        value = packed[a, piece(place(a))]
        for d in range(1, side):
            flight[a][d - 1].wait_recv()
            value = value + parts1[a, d - 1]
        chunk1[a] = value
        flight[a] = [
            send_sum(a, 1, d, chunk1.at[a], parts2.at[a, d - 1], 1 - a) for d in range(1, side)
        ]

    def sum_gather(a):
        value = chunk1[a]
        for d in range(1, side):
            flight[a][d - 1].wait_recv()
            value = value + parts2[a, d - 1]
        chunk2[a] = value
        flight[a] = [
            send_sum(a, 2, d, chunk2.at[a], full.at[a, piece(place(a))], a)
            for d in range(1, side)
        ]
        full[a, piece(place(a))] = value

    def finish(a):
        for copy in flight[a]:
            copy.wait_recv()
        first = 0.5 * full[a, :half]
        second = 0.5 * full[a, half : 2 * half]
        cross = full[a, 2 * half :]
        none = jnp.zeros_like(first)
        lower = jnp.concatenate(
            [jnp.where(left, first, none), jnp.where(left, cross, first)], axis=0
        )
        upper = jnp.concatenate(
            [jnp.where(left, second, cross), jnp.where(left, none, second)], axis=0
        )
        grams, scales = [], []
        for i, triangle in enumerate((lower, upper)):
            gram = triangle + triangle.T
            trace = jnp.sum(gram * eye, axis=(0, 1), keepdims=True)
            inverse = 1.0 / (jnp.sqrt(trace) + 1e-07)
            grams.append(gram * inverse * inverse)
            count = jnp.full((1, 1), counts[replica * mats + 2 * a + i], jnp.int32)
            scales.append(0.2 * jnp.sqrt(count.astype(F32)) * inverse)
        for i, whole in enumerate(polynomials(grams, eye)):
            j = 2 * a + i
            high, low = split(whole)
            r = rounded[j]
            value = jnp.dot(
                jnp.concatenate([r, r], axis=1),
                jnp.concatenate([high, low], axis=0),
                preferred_element_type=F32,
            )
            result[j] = (value * scales[i]).astype(BF16)
            out = pltpu.make_async_copy(result.at[j], update.at[j], out_sem.at[mats + j])
            out.start()
            outs.append(out)

    early, late = (0, 1), (2, 3)
    far = ring // 2
    ring_step(far, early)
    ring_step(far - 1, early)
    ring_step(far, late)
    ring_step(far - 2, early)
    ring_step(far - 1, late)
    ring_step(far - 3, early)
    ring_step(far - 2, late)
    load_mom.wait()
    load_counts.wait()
    sum_scatter(0, *[finish_sum(j) for j in early])
    ring_step(far - 3, late)
    sum_across(0)
    sum_scatter(1, *[finish_sum(j) for j in late])
    sum_gather(0)
    sum_across(1)
    finish(0)
    sum_gather(1)
    finish(1)

    for copy in list(exchange.values()) + list(hop.values()) + sends:
        copy.wait_send()
    for out in outs:
        out.wait()


def solution(mesh):
    ring = mesh.shape["replica"] // 2
    side = 8

    def per_device(grad_part, momentum, row_counts):
        mats, rows, cols = momentum.shape
        slots = ring_messages(ring, mats)
        part = 3 * cols // 2 // side
        pairs = mats // 2
        messages = pairs * 3 * (side - 1)
        block = (mats, rows, cols)
        dma = pltpu.SemaphoreType.DMA
        return pl.pallas_call(
            functools.partial(kernel, ring, side, slots),
            out_shape=(
                jax.ShapeDtypeStruct(block, F32),
                jax.ShapeDtypeStruct(block, BF16),
            ),
            in_specs=[pl.BlockSpec(memory_space=pl.ANY)] * 3,
            out_specs=[pl.BlockSpec(memory_space=pl.ANY)] * 2,
            scratch_shapes=[
                pltpu.VMEM((ring,) + block, BF16),
                pltpu.VMEM((ring,) + block, BF16),
                pltpu.VMEM((len(slots), rows, cols), BF16),
                pltpu.VMEM((len(slots), rows, cols), BF16),
                pltpu.VMEM(block, F32),
                pltpu.VMEM(block, F32),
                pltpu.VMEM(block, BF16),
                pltpu.VMEM(block, BF16),
                pltpu.SMEM(row_counts.shape, jnp.int32),
                pltpu.VMEM((pairs, 3 * cols // 2, cols), F32),
                pltpu.VMEM((pairs, side - 1, part, cols), F32),
                pltpu.VMEM((pairs, part, cols), F32),
                pltpu.VMEM((pairs, side - 1, part, cols), F32),
                pltpu.VMEM((pairs, part, cols), F32),
                pltpu.VMEM((pairs, 3 * cols // 2, cols), F32),
                dma((ring + 2,)),
                dma((2 * mats,)),
                dma((ring,)),
                dma((ring,)),
                dma((len(slots),)),
                dma((len(slots),)),
                dma((messages,)),
                dma((messages,)),
            ],
            compiler_params=pltpu.CompilerParams(
                collective_id=0, has_side_effects=True, vmem_limit_bytes=32 * 1024 * 1024
            ),
        )(grad_part, momentum, row_counts)

    return jax.shard_map(
        per_device,
        mesh=mesh,
        in_specs=(P("replica", None, "fsdp", None), P("replica", "fsdp", None), P()),
        out_specs=(P("replica", "fsdp", None), P("replica", "fsdp", None)),
        check_vma=False,
    )
```

time: 231 us -> 67.3 us (0.29)
  the two profiles are of different devices: /device:TPU:118 before, /device:TPU:16 now
where the time goes in v1:
time: 67.3 us; the launch traced here: 67.1 us
  Pallas kernels  62 us (92%)
  local copies, waits for them, and re-layouts  4.42 us (7%)
    pallas_call x1, Pallas kernels, per_device(): pl.pallas_call(functools.partial(kernel, ring, side, slots), out_shape=(j...  62 us
    unnamed x8, local copies, waits for them, and re-layouts  4.42 us

profile of v1, /device:TPU:16, one launch (start us, length us, event | category | flops | bytes accessed | tf_op | source)
XLA Modules:
  0.0 67.1 jit_solution(18061625524915034575)
XLA Ops:
  0.6 0.0 copy-start
  0.6 1.5 %copy-done = bf16[1,64,112,128]{3,2,1,0:T(8,128)(2,1)S(1)} copy-done((bf16[1,64,112,128]{3,2,1,0:T(8,128)(2,1)S(1)}, bf16[1,64,112,128]{3,2,1,0:T(8,128)(2,1)}, u32[]{:S(2)}) %copy-start) | copy-done | bytes 1835032
  2.1 0.0 copy-start.1
  2.1 0.9 %copy-done.1 = f32[4,112,128]{2,1,0:T(8,128)S(1)} copy-done((f32[4,112,128]{2,1,0:T(8,128)S(1)}, f32[4,112,128]{2,1,0:T(8,128)}, u32[]{:S(2)}) %copy-start.1) | copy-done | bytes 229400
  3.1 0.0 copy-start.2
  3.1 0.7 copy-done.2
  3.7 62.0 %shard_map.50 = (f32[4,112,128]{2,1,0:T(8,128)S(1)}, bf16[4,112,128]{2,1,0:T(8,128)(2,1)S(1)}) custom-call(bf16[1,64,112,128]{3,2,1,0:T(8,128)(2,1)S(1)} %copy-done, f32[4,112,128]{2,1,0:T(8,128)S(1)} %copy-done.1, s32[64]{0:T(128)S(1)} %copy-done.2), custom_call_target="tpu_custom_call" | custom-call | tf_op jit(solution)/shard_map/pallas_call | solution.py:335
  65.8 0.7 %copy.7 = f32[4,112,128]{2,1,0:T(8,128)} copy(f32[4,112,128]{2,1,0:T(8,128)S(1)} %get-tuple-element.4) | data formatting | bytes 458752
  66.4 0.6 copy.8
Async XLA Ops:
  0.6 1.5 %copy-start = (bf16[1,64,112,128]{3,2,1,0:T(8,128)(2,1)S(1)}, bf16[1,64,112,128]{3,2,1,0:T(8,128)(2,1)}, u32[]{:S(2)}) copy-start(bf16[1,64,112,128]{3,2,1,0:T(8,128)(2,1)} %grad.1) | copy-start | bytes 5505028
  2.1 0.9 %copy-start.1 = (f32[4,112,128]{2,1,0:T(8,128)S(1)}, f32[4,112,128]{2,1,0:T(8,128)}, u32[]{:S(2)}) copy-start(f32[4,112,128]{2,1,0:T(8,128)} %momentum.1) | copy-start | bytes 688132
  3.1 0.7 copy-start.2

commit v2 on v1

--- a/solution.py
+++ b/solution.py
@@ -12,6 +12,21 @@
 F32 = jnp.float32
 BF16 = jnp.bfloat16
 COEF = (3.4445, -4.775, 2.0315)
+
+
+THREE_STEPS = {4: 2, 3: 2, 2: 1, 1: 0}
+TWO_STEPS = {4: 2, 3: 2, 2: 0, 1: 0}
+ROUTES = (THREE_STEPS, THREE_STEPS, TWO_STEPS, TWO_STEPS)
+ORDER = (
+    (4, (0, 1)),
+    (3, (0, 1)),
+    (4, (2, 3)),
+    (3, (2, 3)),
+    (2, (0, 1)),
+    (1, (2, 3)),
+    (2, (2, 3)),
+    (1, (0, 1)),
+)
 
 
 def ring_messages(ring, mats):
@@ -39,16 +54,27 @@
     )
 
 
-def polynomials(grams, eye):
+def iterate(rows, grams, eye):
     total = None
     for step in range(ITERS):
         squares = [product(g, g) for g in grams]
         factors = [COEF[0] * eye + COEF[1] * g + COEF[2] * s for g, s in zip(grams, squares)]
-        if step < ITERS - 1:
-            halves = [product(g, f) for g, f in zip(grams, factors)]
-            grams = [product(h, f) for h, f in zip(halves, factors)]
+        if step == ITERS - 1:
+            break
+        halves = [product(g, f) for g, f in zip(grams, factors)]
+        grams = [product(h, f) for h, f in zip(halves, factors)]
         total = factors if total is None else [product(t, f) for t, f in zip(total, factors)]
-    return total
+    partly = []
+    for r, t in zip(rows, total):
+        high, low = split(t)
+        partly.append(
+            jnp.dot(
+                jnp.concatenate([r, r], axis=1),
+                jnp.concatenate([high, low], axis=0),
+                preferred_element_type=F32,
+            )
+        )
+    return [product(p, f) for p, f in zip(partly, factors)]
 
 
 def kernel(
@@ -92,17 +118,17 @@
     y, core = replica // 2, lax.rem(replica, 2)
     x, z = fsdp // side, lax.rem(fsdp, side)
     sibling = (2 * y + 1 - core, fsdp)
-    ahead = (2 * lax.rem(y + 1, ring) + core, fsdp)
-    behind = (2 * lax.rem(y + ring - 1, ring) + core, fsdp)
 
     def along(axis, d):
         if axis == 0:
             return (replica, lax.rem(x + d, side) * side + z)
         return (replica, x * side + lax.rem(z + d, side))
 
+    far_first = sorted(range(1, side), key=lambda d: -min(d, side - d))
     barrier = pltpu.get_barrier_semaphore()
-    peers = [sibling, ahead, behind]
-    peers += [along(axis, d) for axis in (0, 1) for d in range(1, side)]
+    peers = [sibling]
+    peers += [(2 * lax.rem(y + d, ring) + core, fsdp) for d in (1, 2, ring - 2, ring - 1)]
+    peers += [along(axis, d) for d in far_first for axis in (0, 1)]
     for peer in peers:
         pl.semaphore_signal(barrier, inc=1, device_id=peer, device_id_type=MESH)
 
@@ -150,27 +176,32 @@
 
     hop = {}
 
-    def ring_step(hops, chosen):
-        for j in chosen:
-            for way in (0, 1):
-                slot = slots.get((way, hops, j))
-                if slot is None:
-                    continue
-                value = pair_sum(hops if way == 0 else ring - hops, j)
-                before = slots.get((way, hops + 1, j))
-                if before is not None:
-                    hop[before].wait_recv()
-                    value = value + landed[before].astype(F32)
-                stage[slot] = value.astype(BF16)
-                hop[slot] = pltpu.make_async_remote_copy(
-                    src_ref=stage.at[slot],
-                    dst_ref=landed.at[slot],
-                    send_sem=ring_send.at[slot],
-                    recv_sem=ring_recv.at[slot],
-                    device_id=(ahead, behind)[way],
-                    device_id_type=MESH,
-                )
-                hop[slot].start()
+    def arrivals(way, hops, j, value):
+        for before, after in ROUTES[j].items():
+            slot = slots.get((way, before, j))
+            if after == hops and slot is not None:
+                hop[slot].wait_recv()
+                value = value + landed[slot].astype(F32)
+        return value
+
+    def ring_step(hops, j):
+        for way in (0, 1):
+            slot = slots.get((way, hops, j))
+            if slot is None:
+                continue
+            value = arrivals(way, hops, j, pair_sum(hops if way == 0 else ring - hops, j))
+            stage[slot] = value.astype(BF16)
+            step = hops - ROUTES[j][hops]
+            to = lax.rem(y + (step if way == 0 else ring - step), ring)
+            hop[slot] = pltpu.make_async_remote_copy(
+                src_ref=stage.at[slot],
+                dst_ref=landed.at[slot],
+                send_sem=ring_send.at[slot],
+                recv_sem=ring_recv.at[slot],
+                device_id=(2 * to + core, fsdp),
+                device_id_type=MESH,
+            )
+            hop[slot].start()
 
     outs = []
     row = fsdp * rows + lax.broadcasted_iota(jnp.int32, (rows, cols), 0)
@@ -184,9 +215,7 @@
     def finish_sum(j):
         value = pair_sum(0, j)
         for way in (0, 1):
-            slot = slots[way, 1, j]
-            hop[slot].wait_recv()
-            value = value + landed[slot].astype(F32)
+            value = arrivals(way, 0, j, value)
         moved = jnp.where(row < counts[replica * mats + j], 0.95 * mom[j] + value, 0.0)
         new_mom[j] = moved
         out = pltpu.make_async_copy(new_mom.at[j], new_momentum.at[j], out_sem.at[j])
@@ -224,8 +253,8 @@
         packed[a, :half] = jnp.where(left, first[:half], first[half:])
         packed[a, half : 2 * half] = jnp.where(left, second[:half], second[half:])
         packed[a, 2 * half :] = jnp.where(left, first[half:], second[:half])
-        flight[a] = [
-            send_sum(
+        flight[a] = {
+            d: send_sum(
                 a,
                 0,
                 d,
@@ -233,33 +262,32 @@
                 parts1.at[a, d - 1],
                 a,
             )
-            for d in range(1, side)
-        ]
+            for d in far_first
+        }
 
     def sum_across(a):
         value = packed[a, piece(place(a))]
-        for d in range(1, side):
-            flight[a][d - 1].wait_recv()
+        for d in reversed(far_first):
+            flight[a][d].wait_recv()
             value = value + parts1[a, d - 1]
         chunk1[a] = value
-        flight[a] = [
-            send_sum(a, 1, d, chunk1.at[a], parts2.at[a, d - 1], 1 - a) for d in range(1, side)
-        ]
+        flight[a] = {
+            d: send_sum(a, 1, d, chunk1.at[a], parts2.at[a, d - 1], 1 - a) for d in far_first
+        }
 
     def sum_gather(a):
         value = chunk1[a]
-        for d in range(1, side):
-            flight[a][d - 1].wait_recv()
+        for d in reversed(far_first):
+            flight[a][d].wait_recv()
             value = value + parts2[a, d - 1]
         chunk2[a] = value
-        flight[a] = [
-            send_sum(a, 2, d, chunk2.at[a], full.at[a, piece(place(a))], a)
-            for d in range(1, side)
-        ]
+        flight[a] = {
+            d: send_sum(a, 2, d, chunk2.at[a], full.at[a, piece(place(a))], a) for d in far_first
+        }
         full[a, piece(place(a))] = value
 
-    def finish(a):
-        for copy in flight[a]:
+    def whole_grams(a):
+        for copy in flight[a].values():
             copy.wait_recv()
         first = 0.5 * full[a, :half]
         second = 0.5 * full[a, half : 2 * half]
@@ -271,48 +299,33 @@
         upper = jnp.concatenate(
             [jnp.where(left, second, cross), jnp.where(left, none, second)], axis=0
         )
-        grams, scales = [], []
-        for i, triangle in enumerate((lower, upper)):
-            gram = triangle + triangle.T
-            trace = jnp.sum(gram * eye, axis=(0, 1), keepdims=True)
-            inverse = 1.0 / (jnp.sqrt(trace) + 1e-07)
-            grams.append(gram * inverse * inverse)
-            count = jnp.full((1, 1), counts[replica * mats + 2 * a + i], jnp.int32)
-            scales.append(0.2 * jnp.sqrt(count.astype(F32)) * inverse)
-        for i, whole in enumerate(polynomials(grams, eye)):
-            j = 2 * a + i
-            high, low = split(whole)
-            r = rounded[j]
-            value = jnp.dot(
-                jnp.concatenate([r, r], axis=1),
-                jnp.concatenate([high, low], axis=0),
-                preferred_element_type=F32,
-            )
-            result[j] = (value * scales[i]).astype(BF16)
-            out = pltpu.make_async_copy(result.at[j], update.at[j], out_sem.at[mats + j])
-            out.start()
-            outs.append(out)
-
-    early, late = (0, 1), (2, 3)
-    far = ring // 2
-    ring_step(far, early)
-    ring_step(far - 1, early)
-    ring_step(far, late)
-    ring_step(far - 2, early)
-    ring_step(far - 1, late)
-    ring_step(far - 3, early)
-    ring_step(far - 2, late)
+        return [lower + lower.T, upper + upper.T]
+
+    for hops, chosen in ORDER:
+        for j in chosen:
+            ring_step(hops, j)
     load_mom.wait()
     load_counts.wait()
-    sum_scatter(0, *[finish_sum(j) for j in early])
-    ring_step(far - 3, late)
-    sum_across(0)
-    sum_scatter(1, *[finish_sum(j) for j in late])
-    sum_gather(0)
-    sum_across(1)
-    finish(0)
-    sum_gather(1)
-    finish(1)
+    pairs = range(mats // 2)
+    for a in pairs:
+        sum_scatter(a, finish_sum(2 * a), finish_sum(2 * a + 1))
+    for a in pairs:
+        sum_across(a)
+    for a in pairs:
+        sum_gather(a)
+
+    grams, scales = [], []
+    for j, gram in enumerate(whole_grams(0) + whole_grams(1)):
+        trace = jnp.sum(gram * eye, axis=(0, 1), keepdims=True)
+        inverse = 1.0 / (jnp.sqrt(trace) + 1e-07)
+        grams.append(gram * inverse * inverse)
+        count = jnp.full((1, 1), counts[replica * mats + j], jnp.int32)
+        scales.append(0.2 * jnp.sqrt(count.astype(F32)) * inverse)
+    for j, value in enumerate(iterate([rounded[j] for j in range(mats)], grams, eye)):
+        result[j] = (value * scales[j]).astype(BF16)
+        out = pltpu.make_async_copy(result.at[j], update.at[j], out_sem.at[mats + j])
+        out.start()
+        outs.append(out)
 
     for copy in list(exchange.values()) + list(hop.values()) + sends:
         copy.wait_send()
@@ -366,7 +379,7 @@
                 dma((messages,)),
             ],
             compiler_params=pltpu.CompilerParams(
-                collective_id=0, has_side_effects=True, vmem_limit_bytes=32 * 1024 * 1024
+                collective_id=0, has_side_effects=True, vmem_limit_bytes=60 * 1024 * 1024
             ),
         )(grad_part, momentum, row_counts)
 

time: 67.3 us -> 60 us (0.89)
  the two profiles are of different devices: /device:TPU:16 before, /device:TPU:1 now
where the time goes in v2:
time: 60 us; the launch traced here: 59.6 us
  Pallas kernels  55.8 us (93%)
  local copies, waits for them, and re-layouts  3.19 us (5%)
  between operations  0.64 us (1%)
    pallas_call x1, Pallas kernels, per_device(): pl.pallas_call(functools.partial(kernel, ring, side, slots), out_shape=(j...  55.8 us
    unnamed x2, local copies, waits for them, and re-layouts  3.19 us

profile of v2, /device:TPU:1, one launch (start us, length us, event | category | flops | bytes accessed | tf_op | source)
XLA Modules:
  0.0 59.6 jit_solution(1565409534879369565)
XLA Ops:
  0.6 55.8 %shard_map.50 = (f32[4,112,128]{2,1,0:T(8,128)}, bf16[4,112,128]{2,1,0:T(8,128)(2,1)}) custom-call(bf16[1,64,112,128]{3,2,1,0:T(8,128)(2,1)} %grad.1, f32[4,112,128]{2,1,0:T(8,128)} %momentum.1, s32[64]{0:T(128)} %row_counts.1), custom_call_target="tpu_custom_call" | custom-call | tf_op jit(solution)/shard_map/pallas_call | solution.py:348
  56.4 1.6 %copy.7 = f32[4,112,128]{2,1,0:T(8,128)} copy(f32[4,112,128]{2,1,0:T(8,128)} %get-tuple-element.4) | data formatting | bytes 458752
  58.1 1.6 %copy.8 = bf16[4,112,128]{2,1,0:T(8,128)(2,1)} copy(bf16[4,112,128]{2,1,0:T(8,128)(2,1)} %get-tuple-element.5) | data formatting | bytes 229376

commit v3 on v2

--- a/solution.py
+++ b/solution.py
@@ -91,9 +91,7 @@
     stage,
     landed,
     mom,
-    new_mom,
     rounded,
-    result,
     counts,
     packed,
     parts1,
@@ -102,7 +100,6 @@
     chunk2,
     full,
     load_sem,
-    out_sem,
     sib_send,
     sib_recv,
     ring_send,
@@ -203,7 +200,6 @@
             )
             hop[slot].start()
 
-    outs = []
     row = fsdp * rows + lax.broadcasted_iota(jnp.int32, (rows, cols), 0)
     lane = lax.broadcasted_iota(jnp.int32, (half, cols), 1)
     left = lane < half
@@ -217,15 +213,16 @@
         for way in (0, 1):
             value = arrivals(way, 0, j, value)
         moved = jnp.where(row < counts[replica * mats + j], 0.95 * mom[j] + value, 0.0)
-        new_mom[j] = moved
-        out = pltpu.make_async_copy(new_mom.at[j], new_momentum.at[j], out_sem.at[j])
-        out.start()
-        outs.append(out)
+        new_momentum[j] = moved
         r = moved.astype(BF16)
         rounded[j] = r
         return lax.dot_general(r, r, (((0,), (0,)), ((), ())), preferred_element_type=F32)
 
     sends = []
+
+    def sent():
+        while len(sends) > mats // 2 * (side - 1):
+            sends.pop(0).wait_send()
 
     def send_sum(a, phase, d, src, dst, axis):
         at = (a * 3 + phase) * (side - 1) + d - 1
@@ -309,10 +306,14 @@
     pairs = range(mats // 2)
     for a in pairs:
         sum_scatter(a, finish_sum(2 * a), finish_sum(2 * a + 1))
+    for copy in list(exchange.values()) + list(hop.values()):
+        copy.wait_send()
     for a in pairs:
         sum_across(a)
+    sent()
     for a in pairs:
         sum_gather(a)
+    sent()
 
     grams, scales = [], []
     for j, gram in enumerate(whole_grams(0) + whole_grams(1)):
@@ -322,15 +323,10 @@
         count = jnp.full((1, 1), counts[replica * mats + j], jnp.int32)
         scales.append(0.2 * jnp.sqrt(count.astype(F32)) * inverse)
     for j, value in enumerate(iterate([rounded[j] for j in range(mats)], grams, eye)):
-        result[j] = (value * scales[j]).astype(BF16)
-        out = pltpu.make_async_copy(result.at[j], update.at[j], out_sem.at[mats + j])
-        out.start()
-        outs.append(out)
-
-    for copy in list(exchange.values()) + list(hop.values()) + sends:
+        update[j] = (value * scales[j]).astype(BF16)
+
+    for copy in sends:
         copy.wait_send()
-    for out in outs:
-        out.wait()
 
 
 def solution(mesh):
@@ -348,19 +344,17 @@
         return pl.pallas_call(
             functools.partial(kernel, ring, side, slots),
             out_shape=(
-                jax.ShapeDtypeStruct(block, F32),
-                jax.ShapeDtypeStruct(block, BF16),
+                pltpu.VMEM(block, F32),
+                pltpu.VMEM(block, BF16),
             ),
-            in_specs=[pl.BlockSpec(memory_space=pl.ANY)] * 3,
-            out_specs=[pl.BlockSpec(memory_space=pl.ANY)] * 2,
+            in_specs=[pl.BlockSpec(memory_space=pltpu.HBM)] * 3,
+            out_specs=[pl.BlockSpec(memory_space=pltpu.VMEM)] * 2,
             scratch_shapes=[
                 pltpu.VMEM((ring,) + block, BF16),
                 pltpu.VMEM((ring,) + block, BF16),
                 pltpu.VMEM((len(slots), rows, cols), BF16),
                 pltpu.VMEM((len(slots), rows, cols), BF16),
                 pltpu.VMEM(block, F32),
-                pltpu.VMEM(block, F32),
-                pltpu.VMEM(block, BF16),
                 pltpu.VMEM(block, BF16),
                 pltpu.SMEM(row_counts.shape, jnp.int32),
                 pltpu.VMEM((pairs, 3 * cols // 2, cols), F32),
@@ -370,7 +364,6 @@
                 pltpu.VMEM((pairs, part, cols), F32),
                 pltpu.VMEM((pairs, 3 * cols // 2, cols), F32),
                 dma((ring + 2,)),
-                dma((2 * mats,)),
                 dma((ring,)),
                 dma((ring,)),
                 dma((len(slots),)),

time: 60 us -> 57.4 us (0.957)
  local copies, waits for them, and re-layouts: 3.19 us -> 1.34 us
  Pallas kernels: 55.8 us -> 55.1 us
    unnamed x2, local copies, waits for them, and re-layouts: 3.19 us -> 1.34 us
    pallas_call x1, Pallas kernels: 55.8 us -> 55.1 us  [per_device(): pl.pallas_call(functools.partial(kernel, ring, side, slots), out_shape=(p...]
where the time goes in v3:
time: 57.4 us; the launch traced here: 57.1 us
  Pallas kernels  55.1 us (96%)
  local copies, waits for them, and re-layouts  1.34 us (2%)
  between operations  0.64 us (1%)
    pallas_call x1, Pallas kernels, per_device(): pl.pallas_call(functools.partial(kernel, ring, side, slots), out_shape=(p...  55.1 us
    unnamed x2, local copies, waits for them, and re-layouts  1.34 us

profile of v3, /device:TPU:1, one launch (start us, length us, event | category | flops | bytes accessed | tf_op | source)
XLA Modules:
  0.0 57.1 jit_solution(5047099416740661780)
XLA Ops:
  0.6 55.1 %shard_map.50 = (f32[4,112,128]{2,1,0:T(8,128)S(1)}, bf16[4,112,128]{2,1,0:T(8,128)(2,1)S(1)}) custom-call(bf16[1,64,112,128]{3,2,1,0:T(8,128)(2,1)} %grad.1, f32[4,112,128]{2,1,0:T(8,128)} %momentum.1, s32[64]{0:T(128)} %row_counts.1), custom_call_target="tpu_custom_call" | custom-call | tf_op jit(solution)/shard_map/pallas_call | solution.py:344
  55.8 0.7 %copy.7 = f32[4,112,128]{2,1,0:T(8,128)} copy(f32[4,112,128]{2,1,0:T(8,128)S(1)} %get-tuple-element.2) | data formatting | bytes 458752
  56.5 0.6 %copy.8 = bf16[4,112,128]{2,1,0:T(8,128)(2,1)} copy(bf16[4,112,128]{2,1,0:T(8,128)(2,1)S(1)} %get-tuple-element.3) | data formatting | bytes 229376

commit v4 on v3

--- a/solution.py
+++ b/solution.py
@@ -104,30 +104,44 @@
     sib_recv,
     ring_send,
     ring_recv,
-    sum_send,
-    sum_recv,
+    send1,
+    recv1,
+    send2,
+    recv2,
+    send3,
+    recv3,
 ):
     mats, rows, cols = mom.shape
-    half = cols // 2
-    part = chunk1.shape[1]
+    strip = cols // side
     replica = lax.axis_index("replica")
     fsdp = lax.axis_index("fsdp")
     y, core = replica // 2, lax.rem(replica, 2)
     x, z = fsdp // side, lax.rem(fsdp, side)
     sibling = (2 * y + 1 - core, fsdp)
 
-    def along(axis, d):
+    def along(axis, d, which):
         if axis == 0:
-            return (replica, lax.rem(x + d, side) * side + z)
-        return (replica, x * side + lax.rem(z + d, side))
+            return (2 * y + which, lax.rem(x + d, side) * side + z)
+        return (2 * y + which, x * side + lax.rem(z + d, side))
 
     far_first = sorted(range(1, side), key=lambda d: -min(d, side - d))
     barrier = pltpu.get_barrier_semaphore()
-    peers = [sibling]
-    peers += [(2 * lax.rem(y + d, ring) + core, fsdp) for d in (1, 2, ring - 2, ring - 1)]
-    peers += [along(axis, d) for d in far_first for axis in (0, 1)]
-    for peer in peers:
+
+    def greet(peer):
         pl.semaphore_signal(barrier, inc=1, device_id=peer, device_id_type=MESH)
+
+    steps = (1, 2, ring - 2, ring - 1)
+    greet(sibling)
+    for d in steps:
+        greet((2 * lax.rem(y + d, ring) + core, fsdp))
+    lines = [(axis, d) for d in far_first for axis in (0, 1)]
+    for axis, d in lines:
+        greet(along(axis, d, 1))
+
+    @pl.when(core == 1)
+    def _():
+        for axis, d in lines:
+            greet(along(axis, d, 0))
 
     order = [ring // 2]
     for hops in range(ring // 2 - 1, 0, -1):
@@ -148,7 +162,7 @@
     load_counts = pltpu.make_async_copy(row_counts, counts, load_sem.at[ring + 1])
     load_counts.start()
 
-    pl.semaphore_wait(barrier, len(peers))
+    pl.semaphore_wait(barrier, 1 + len(steps) + (1 + core) * len(lines))
 
     exchange = {}
     for o in order:
@@ -201,12 +215,9 @@
             hop[slot].start()
 
     row = fsdp * rows + lax.broadcasted_iota(jnp.int32, (rows, cols), 0)
-    lane = lax.broadcasted_iota(jnp.int32, (half, cols), 1)
-    left = lane < half
-    eye = (
-        lax.broadcasted_iota(jnp.int32, (cols, cols), 0)
-        == lax.broadcasted_iota(jnp.int32, (cols, cols), 1)
-    ).astype(F32)
+    down = lax.broadcasted_iota(jnp.int32, (cols, cols), 0)
+    across = lax.broadcasted_iota(jnp.int32, (cols, cols), 1)
+    eye = (down == across).astype(F32)
 
     def finish_sum(j):
         value = pair_sum(0, j)
@@ -218,85 +229,64 @@
         rounded[j] = r
         return lax.dot_general(r, r, (((0,), (0,)), ((), ())), preferred_element_type=F32)
 
-    sends = []
-
-    def sent():
-        while len(sends) > mats // 2 * (side - 1):
-            sends.pop(0).wait_send()
-
-    def send_sum(a, phase, d, src, dst, axis):
-        at = (a * 3 + phase) * (side - 1) + d - 1
-        copy = pltpu.make_async_remote_copy(
+    def place(axis):
+        return x if axis == 0 else z
+
+    def remote(src, dst, send_sem, recv_sem, to):
+        return pltpu.make_async_remote_copy(
             src_ref=src,
             dst_ref=dst,
-            send_sem=sum_send.at[at],
-            recv_sem=sum_recv.at[at],
-            device_id=along(axis, d),
+            send_sem=send_sem,
+            recv_sem=recv_sem,
+            device_id=to,
             device_id_type=MESH,
         )
-        copy.start()
-        sends.append(copy)
-        return copy
-
-    def piece(index):
-        return pl.ds(pl.multiple_of(index * part, 8), part)
-
-    flight = {}
-
-    def place(axis):
-        return x if axis == 0 else z
-
-    def sum_scatter(a, first, second):
-        packed[a, :half] = jnp.where(left, first[:half], first[half:])
-        packed[a, half : 2 * half] = jnp.where(left, second[:half], second[half:])
-        packed[a, 2 * half :] = jnp.where(left, first[half:], second[:half])
-        flight[a] = {
-            d: send_sum(
-                a,
-                0,
-                d,
-                packed.at[a, piece(lax.rem(place(a) + d, side))],
-                parts1.at[a, d - 1],
-                a,
-            )
-            for d in far_first
-        }
-
-    def sum_across(a):
-        value = packed[a, piece(place(a))]
-        for d in reversed(far_first):
-            flight[a][d].wait_recv()
-            value = value + parts1[a, d - 1]
-        chunk1[a] = value
-        flight[a] = {
-            d: send_sum(a, 1, d, chunk1.at[a], parts2.at[a, d - 1], 1 - a) for d in far_first
-        }
-
-    def sum_gather(a):
-        value = chunk1[a]
-        for d in reversed(far_first):
-            flight[a][d].wait_recv()
-            value = value + parts2[a, d - 1]
-        chunk2[a] = value
-        flight[a] = {
-            d: send_sum(a, 2, d, chunk2.at[a], full.at[a, piece(place(a))], a) for d in far_first
-        }
-        full[a, piece(place(a))] = value
-
-    def whole_grams(a):
-        for copy in flight[a].values():
-            copy.wait_recv()
-        first = 0.5 * full[a, :half]
-        second = 0.5 * full[a, half : 2 * half]
-        cross = full[a, 2 * half :]
-        none = jnp.zeros_like(first)
-        lower = jnp.concatenate(
-            [jnp.where(left, first, none), jnp.where(left, cross, first)], axis=0
-        )
-        upper = jnp.concatenate(
-            [jnp.where(left, second, cross), jnp.where(left, none, second)], axis=0
-        )
-        return [lower + lower.T, upper + upper.T]
+
+    def to_owner(a, d):
+        return remote(
+            packed.at[a, lax.rem(place(a) + d, side)],
+            parts1.at[core, a, d],
+            send1.at[a, d],
+            recv1.at[core, a, d],
+            along(a, d, 1),
+        )
+
+    def from_partner(which, a, d):
+        return remote(
+            packed.at[a, 0],
+            parts1.at[which, a, d],
+            send1.at[a, d],
+            recv1.at[which, a, d],
+            along(a, d, 1),
+        )
+
+    def across_owners(a, d):
+        return remote(
+            chunk1.at[a], parts2.at[a, d - 1], send2.at[a, d], recv2.at[a, d], along(1 - a, d, 1)
+        )
+
+    def to_user(which, a, d):
+        return remote(
+            chunk2.at[a, which],
+            full.at[a, place(a)],
+            send3.at[which, a, d],
+            recv3.at[a, d],
+            along(a, d, which),
+        )
+
+    def pack(a, first, second):
+        tile = jnp.where(down >= across, first, second)
+        diagonal = jnp.sum(second * eye, axis=0, keepdims=True)
+        for index in range(side):
+            packed[a, index, :strip] = tile[index * strip : (index + 1) * strip]
+            packed[a, index, strip:] = diagonal
+
+    def unpack(a):
+        tile = jnp.concatenate([full[a, index, :strip] for index in range(side)], axis=0)
+        turned = tile.T
+        first = jnp.where(down >= across, tile, turned)
+        second = jnp.where(down < across, tile, turned)
+        return [first, jnp.where(down == across, full[a, 0, strip:], second)]
 
     for hops, chosen in ORDER:
         for j in chosen:
@@ -305,18 +295,56 @@
     load_counts.wait()
     pairs = range(mats // 2)
     for a in pairs:
-        sum_scatter(a, finish_sum(2 * a), finish_sum(2 * a + 1))
+        pack(a, finish_sum(2 * a), finish_sum(2 * a + 1))
+        for d in far_first:
+            to_owner(a, d).start()
+
+        @pl.when(core == 0)
+        def _():
+            to_owner(a, 0).start()
+
     for copy in list(exchange.values()) + list(hop.values()):
         copy.wait_send()
+
+    @pl.when(core == 1)
+    def _():
+        for a in pairs:
+            value = packed[a, place(a)]
+            for d in reversed(far_first):
+                from_partner(1, a, d).wait_recv()
+                value = value + parts1[1, a, d]
+            chunk1[a, 1] = value
+            from_partner(0, a, 0).wait_recv()
+            value = parts1[0, a, 0]
+            for d in reversed(far_first):
+                from_partner(0, a, d).wait_recv()
+                value = value + parts1[0, a, d]
+            chunk1[a, 0] = value
+            for d in far_first:
+                across_owners(a, d).start()
+        for a in pairs:
+            value = chunk1[a]
+            for d in reversed(far_first):
+                across_owners(a, d).wait_recv()
+                value = value + parts2[a, d - 1]
+            chunk2[a] = value
+            full[a, place(a)] = value[1]
+            for d in far_first:
+                to_user(0, a, d).start()
+                to_user(1, a, d).start()
+            to_user(0, a, 0).start()
+
+    @pl.when(core == 0)
+    def _():
+        for a in pairs:
+            to_user(0, a, 0).wait_recv()
+
     for a in pairs:
-        sum_across(a)
-    sent()
-    for a in pairs:
-        sum_gather(a)
-    sent()
+        for d in reversed(far_first):
+            to_user(0, a, d).wait_recv()
 
     grams, scales = [], []
-    for j, gram in enumerate(whole_grams(0) + whole_grams(1)):
+    for j, gram in enumerate(unpack(0) + unpack(1)):
         trace = jnp.sum(gram * eye, axis=(0, 1), keepdims=True)
         inverse = 1.0 / (jnp.sqrt(trace) + 1e-07)
         grams.append(gram * inverse * inverse)
@@ -325,8 +353,23 @@
     for j, value in enumerate(iterate([rounded[j] for j in range(mats)], grams, eye)):
         update[j] = (value * scales[j]).astype(BF16)
 
-    for copy in sends:
-        copy.wait_send()
+    for a in pairs:
+        for d in far_first:
+            to_owner(a, d).wait_send()
+
+    @pl.when(core == 0)
+    def _():
+        for a in pairs:
+            to_owner(a, 0).wait_send()
+
+    @pl.when(core == 1)
+    def _():
+        for a in pairs:
+            for d in far_first:
+                across_owners(a, d).wait_send()
+                to_user(0, a, d).wait_send()
+                to_user(1, a, d).wait_send()
+            to_user(0, a, 0).wait_send()
 
 
 def solution(mesh):
@@ -336,9 +379,8 @@
     def per_device(grad_part, momentum, row_counts):
         mats, rows, cols = momentum.shape
         slots = ring_messages(ring, mats)
-        part = 3 * cols // 2 // side
         pairs = mats // 2
-        messages = pairs * 3 * (side - 1)
+        piece = (cols // side + 1, cols)
         block = (mats, rows, cols)
         dma = pltpu.SemaphoreType.DMA
         return pl.pallas_call(
@@ -357,19 +399,23 @@
                 pltpu.VMEM(block, F32),
                 pltpu.VMEM(block, BF16),
                 pltpu.SMEM(row_counts.shape, jnp.int32),
-                pltpu.VMEM((pairs, 3 * cols // 2, cols), F32),
-                pltpu.VMEM((pairs, side - 1, part, cols), F32),
-                pltpu.VMEM((pairs, part, cols), F32),
-                pltpu.VMEM((pairs, side - 1, part, cols), F32),
-                pltpu.VMEM((pairs, part, cols), F32),
-                pltpu.VMEM((pairs, 3 * cols // 2, cols), F32),
+                pltpu.VMEM((pairs, side) + piece, F32),
+                pltpu.VMEM((2, pairs, side) + piece, F32),
+                pltpu.VMEM((pairs, 2) + piece, F32),
+                pltpu.VMEM((pairs, side - 1, 2) + piece, F32),
+                pltpu.VMEM((pairs, 2) + piece, F32),
+                pltpu.VMEM((pairs, side) + piece, F32),
                 dma((ring + 2,)),
                 dma((ring,)),
                 dma((ring,)),
                 dma((len(slots),)),
                 dma((len(slots),)),
-                dma((messages,)),
-                dma((messages,)),
+                dma((pairs, side)),
+                dma((2, pairs, side)),
+                dma((pairs, side)),
+                dma((pairs, side)),
+                dma((2, pairs, side)),
+                dma((pairs, side)),
             ],
             compiler_params=pltpu.CompilerParams(
                 collective_id=0, has_side_effects=True, vmem_limit_bytes=60 * 1024 * 1024

time: 57.4 us -> 57.8 us (level)
  no operation moved by 1% of the time
where the time goes in v4:
time: 57.8 us; the launch traced here: 57.6 us
  Pallas kernels  55.6 us (96%)
  local copies, waits for them, and re-layouts  1.34 us (2%)
  between operations  0.64 us (1%)
    pallas_call x1, Pallas kernels, per_device(): pl.pallas_call(functools.partial(kernel, ring, side, slots), out_shape=(p...  55.6 us
    unnamed x2, local copies, waits for them, and re-layouts  1.34 us

profile of v4, /device:TPU:1, one launch (start us, length us, event | category | flops | bytes accessed | tf_op | source)
XLA Modules:
  0.0 57.6 jit_solution(2953469344433188889)
XLA Ops:
  0.6 55.6 %shard_map.50 = (f32[4,112,128]{2,1,0:T(8,128)S(1)}, bf16[4,112,128]{2,1,0:T(8,128)(2,1)S(1)}) custom-call(bf16[1,64,112,128]{3,2,1,0:T(8,128)(2,1)} %grad.1, f32[4,112,128]{2,1,0:T(8,128)} %momentum.1, s32[64]{0:T(128)} %row_counts.1), custom_call_target="tpu_custom_call" | custom-call | tf_op jit(solution)/shard_map/pallas_call | solution.py:386
  56.3 0.7 %copy.7 = f32[4,112,128]{2,1,0:T(8,128)} copy(f32[4,112,128]{2,1,0:T(8,128)S(1)} %get-tuple-element.2) | data formatting | bytes 458752
  57.0 0.6 %copy.8 = bf16[4,112,128]{2,1,0:T(8,128)(2,1)} copy(bf16[4,112,128]{2,1,0:T(8,128)(2,1)S(1)} %get-tuple-element.3) | data formatting | bytes 229376

commit v5 on v4

--- a/solution.py
+++ b/solution.py
@@ -119,10 +119,10 @@
     x, z = fsdp // side, lax.rem(fsdp, side)
     sibling = (2 * y + 1 - core, fsdp)
 
-    def along(axis, d, which):
+    def along(axis, d):
         if axis == 0:
-            return (2 * y + which, lax.rem(x + d, side) * side + z)
-        return (2 * y + which, x * side + lax.rem(z + d, side))
+            return (replica, lax.rem(x + d, side) * side + z)
+        return (replica, x * side + lax.rem(z + d, side))
 
     far_first = sorted(range(1, side), key=lambda d: -min(d, side - d))
     barrier = pltpu.get_barrier_semaphore()
@@ -136,12 +136,7 @@
         greet((2 * lax.rem(y + d, ring) + core, fsdp))
     lines = [(axis, d) for d in far_first for axis in (0, 1)]
     for axis, d in lines:
-        greet(along(axis, d, 1))
-
-    @pl.when(core == 1)
-    def _():
-        for axis, d in lines:
-            greet(along(axis, d, 0))
+        greet(along(axis, d))
 
     order = [ring // 2]
     for hops in range(ring // 2 - 1, 0, -1):
@@ -162,7 +157,7 @@
     load_counts = pltpu.make_async_copy(row_counts, counts, load_sem.at[ring + 1])
     load_counts.start()
 
-    pl.semaphore_wait(barrier, 1 + len(steps) + (1 + core) * len(lines))
+    pl.semaphore_wait(barrier, 1 + len(steps) + len(lines))
 
     exchange = {}
     for o in order:
@@ -245,33 +240,20 @@
     def to_owner(a, d):
         return remote(
             packed.at[a, lax.rem(place(a) + d, side)],
-            parts1.at[core, a, d],
+            parts1.at[a, d - 1],
             send1.at[a, d],
-            recv1.at[core, a, d],
-            along(a, d, 1),
-        )
-
-    def from_partner(which, a, d):
-        return remote(
-            packed.at[a, 0],
-            parts1.at[which, a, d],
-            send1.at[a, d],
-            recv1.at[which, a, d],
-            along(a, d, 1),
+            recv1.at[a, d],
+            along(a, d),
         )
 
     def across_owners(a, d):
         return remote(
-            chunk1.at[a], parts2.at[a, d - 1], send2.at[a, d], recv2.at[a, d], along(1 - a, d, 1)
-        )
-
-    def to_user(which, a, d):
+            chunk1.at[a], parts2.at[a, d - 1], send2.at[a, d], recv2.at[a, d], along(1 - a, d)
+        )
+
+    def to_user(a, d):
         return remote(
-            chunk2.at[a, which],
-            full.at[a, place(a)],
-            send3.at[which, a, d],
-            recv3.at[a, d],
-            along(a, d, which),
+            chunk2.at[a], full.at[a, place(a)], send3.at[a, d], recv3.at[a, d], along(a, d)
         )
 
     def pack(a, first, second):
@@ -298,50 +280,34 @@
         pack(a, finish_sum(2 * a), finish_sum(2 * a + 1))
         for d in far_first:
             to_owner(a, d).start()
-
-        @pl.when(core == 0)
-        def _():
-            to_owner(a, 0).start()
-
     for copy in list(exchange.values()) + list(hop.values()):
         copy.wait_send()
-
-    @pl.when(core == 1)
-    def _():
-        for a in pairs:
-            value = packed[a, place(a)]
-            for d in reversed(far_first):
-                from_partner(1, a, d).wait_recv()
-                value = value + parts1[1, a, d]
-            chunk1[a, 1] = value
-            from_partner(0, a, 0).wait_recv()
-            value = parts1[0, a, 0]
-            for d in reversed(far_first):
-                from_partner(0, a, d).wait_recv()
-                value = value + parts1[0, a, d]
-            chunk1[a, 0] = value
-            for d in far_first:
-                across_owners(a, d).start()
-        for a in pairs:
-            value = chunk1[a]
-            for d in reversed(far_first):
-                across_owners(a, d).wait_recv()
-                value = value + parts2[a, d - 1]
-            chunk2[a] = value
-            full[a, place(a)] = value[1]
-            for d in far_first:
-                to_user(0, a, d).start()
-                to_user(1, a, d).start()
-            to_user(0, a, 0).start()
-
-    @pl.when(core == 0)
-    def _():
-        for a in pairs:
-            to_user(0, a, 0).wait_recv()
-
-    for a in pairs:
+    for a in pairs:
+        value = packed[a, place(a)]
         for d in reversed(far_first):
-            to_user(0, a, d).wait_recv()
+            to_owner(a, d).wait_recv()
+            value = value + parts1[a, d - 1]
+        chunk1[a] = value
+        for d in far_first:
+            across_owners(a, d).start()
+    for a in pairs:
+        for d in far_first:
+            to_owner(a, d).wait_send()
+    for a in pairs:
+        value = chunk1[a]
+        for d in reversed(far_first):
+            across_owners(a, d).wait_recv()
+            value = value + parts2[a, d - 1]
+        chunk2[a] = value
+        full[a, place(a)] = value
+        for d in far_first:
+            to_user(a, d).start()
+    for a in pairs:
+        for d in far_first:
+            across_owners(a, d).wait_send()
+    for a in pairs:
+        for d in reversed(far_first):
+            to_user(a, d).wait_recv()
 
     grams, scales = [], []
     for j, gram in enumerate(unpack(0) + unpack(1)):
@@ -355,21 +321,7 @@
 
     for a in pairs:
         for d in far_first:
-            to_owner(a, d).wait_send()
-
-    @pl.when(core == 0)
-    def _():
-        for a in pairs:
-            to_owner(a, 0).wait_send()
-
-    @pl.when(core == 1)
-    def _():
-        for a in pairs:
-            for d in far_first:
-                across_owners(a, d).wait_send()
-                to_user(0, a, d).wait_send()
-                to_user(1, a, d).wait_send()
-            to_user(0, a, 0).wait_send()
+            to_user(a, d).wait_send()
 
 
 def solution(mesh):
@@ -400,10 +352,10 @@
                 pltpu.VMEM(block, BF16),
                 pltpu.SMEM(row_counts.shape, jnp.int32),
                 pltpu.VMEM((pairs, side) + piece, F32),
-                pltpu.VMEM((2, pairs, side) + piece, F32),
-                pltpu.VMEM((pairs, 2) + piece, F32),
-                pltpu.VMEM((pairs, side - 1, 2) + piece, F32),
-                pltpu.VMEM((pairs, 2) + piece, F32),
+                pltpu.VMEM((pairs, side - 1) + piece, F32),
+                pltpu.VMEM((pairs,) + piece, F32),
+                pltpu.VMEM((pairs, side - 1) + piece, F32),
+                pltpu.VMEM((pairs,) + piece, F32),
                 pltpu.VMEM((pairs, side) + piece, F32),
                 dma((ring + 2,)),
                 dma((ring,)),
@@ -411,10 +363,10 @@
                 dma((len(slots),)),
                 dma((len(slots),)),
                 dma((pairs, side)),
-                dma((2, pairs, side)),
-                dma((pairs, side)),
-                dma((pairs, side)),
-                dma((2, pairs, side)),
+                dma((pairs, side)),
+                dma((pairs, side)),
+                dma((pairs, side)),
+                dma((pairs, side)),
                 dma((pairs, side)),
             ],
             compiler_params=pltpu.CompilerParams(

time: 57.8 us -> 56.5 us (0.978)
  Pallas kernels: 55.6 us -> 54.3 us
    pallas_call x1, Pallas kernels: 55.6 us -> 54.3 us  [per_device(): pl.pallas_call(functools.partial(kernel, ring, side, slots), out_shape=(p...]
where the time goes in v5:
time: 56.5 us; the launch traced here: 56.3 us
  Pallas kernels  54.3 us (96%)
  local copies, waits for them, and re-layouts  1.34 us (2%)
  between operations  0.64 us (1%)
    pallas_call x1, Pallas kernels, per_device(): pl.pallas_call(functools.partial(kernel, ring, side, slots), out_shape=(p...  54.3 us
    unnamed x2, local copies, waits for them, and re-layouts  1.34 us

profile of v5, /device:TPU:1, one launch (start us, length us, event | category | flops | bytes accessed | tf_op | source)
XLA Modules:
  0.0 56.3 jit_solution(10358481076422249153)
XLA Ops:
  0.6 54.3 %shard_map.50 = (f32[4,112,128]{2,1,0:T(8,128)S(1)}, bf16[4,112,128]{2,1,0:T(8,128)(2,1)S(1)}) custom-call(bf16[1,64,112,128]{3,2,1,0:T(8,128)(2,1)} %grad.1, f32[4,112,128]{2,1,0:T(8,128)} %momentum.1, s32[64]{0:T(128)} %row_counts.1), custom_call_target="tpu_custom_call" | custom-call | tf_op jit(solution)/shard_map/pallas_call | solution.py:338
  55.0 0.7 %copy.7 = f32[4,112,128]{2,1,0:T(8,128)} copy(f32[4,112,128]{2,1,0:T(8,128)S(1)} %get-tuple-element.2) | data formatting | bytes 458752
  55.7 0.6 %copy.8 = bf16[4,112,128]{2,1,0:T(8,128)(2,1)} copy(bf16[4,112,128]{2,1,0:T(8,128)(2,1)S(1)} %get-tuple-element.3) | data formatting | bytes 229376

commit v6 on v5

--- a/solution.py
+++ b/solution.py
@@ -55,10 +55,16 @@
 
 
 def iterate(rows, grams, eye):
+    norms = [jnp.sqrt(jnp.sum(g * eye, axis=(0, 1), keepdims=True)) for g in grams]
+    inverses = [1.0 / (n + 1e-07) for n in norms]
     total = None
     for step in range(ITERS):
         squares = [product(g, g) for g in grams]
-        factors = [COEF[0] * eye + COEF[1] * g + COEF[2] * s for g, s in zip(grams, squares)]
+        if step == 0:
+            scales = [i * i for i in inverses]
+            grams = [s * g for s, g in zip(scales, grams)]
+            squares = [s * (s * h) for s, h in zip(scales, squares)]
+        factors = [COEF[0] * eye + COEF[1] * g + COEF[2] * h for g, h in zip(grams, squares)]
         if step == ITERS - 1:
             break
         halves = [product(g, f) for g, f in zip(grams, factors)]
@@ -74,7 +80,7 @@
                 preferred_element_type=F32,
             )
         )
-    return [product(p, f) for p, f in zip(partly, factors)]
+    return [product(p, f) * i for p, f, i in zip(partly, factors, inverses)]
 
 
 def kernel(
@@ -276,13 +282,13 @@
     load_mom.wait()
     load_counts.wait()
     pairs = range(mats // 2)
-    for a in pairs:
+    for a in reversed(pairs):
         pack(a, finish_sum(2 * a), finish_sum(2 * a + 1))
         for d in far_first:
             to_owner(a, d).start()
     for copy in list(exchange.values()) + list(hop.values()):
         copy.wait_send()
-    for a in pairs:
+    for a in reversed(pairs):
         value = packed[a, place(a)]
         for d in reversed(far_first):
             to_owner(a, d).wait_recv()
@@ -293,7 +299,7 @@
     for a in pairs:
         for d in far_first:
             to_owner(a, d).wait_send()
-    for a in pairs:
+    for a in reversed(pairs):
         value = chunk1[a]
         for d in reversed(far_first):
             across_owners(a, d).wait_recv()
@@ -309,15 +315,10 @@
         for d in reversed(far_first):
             to_user(a, d).wait_recv()
 
-    grams, scales = [], []
-    for j, gram in enumerate(unpack(0) + unpack(1)):
-        trace = jnp.sum(gram * eye, axis=(0, 1), keepdims=True)
-        inverse = 1.0 / (jnp.sqrt(trace) + 1e-07)
-        grams.append(gram * inverse * inverse)
+    values = iterate([rounded[j] for j in range(mats)], unpack(0) + unpack(1), eye)
+    for j, value in enumerate(values):
         count = jnp.full((1, 1), counts[replica * mats + j], jnp.int32)
-        scales.append(0.2 * jnp.sqrt(count.astype(F32)) * inverse)
-    for j, value in enumerate(iterate([rounded[j] for j in range(mats)], grams, eye)):
-        update[j] = (value * scales[j]).astype(BF16)
+        update[j] = (value * (0.2 * jnp.sqrt(count.astype(F32)))).astype(BF16)
 
     for a in pairs:
         for d in far_first:

time: 56.5 us -> 55.3 us (0.979)
  Pallas kernels: 54.3 us -> 52.9 us
    pallas_call x1, Pallas kernels: 54.3 us -> 52.9 us  [per_device(): pl.pallas_call(functools.partial(kernel, ring, side, slots), out_shape=(p...]
where the time goes in v6:
time: 55.3 us; the launch traced here: 54.8 us
  Pallas kernels  52.9 us (96%)
  local copies, waits for them, and re-layouts  1.34 us (2%)
  between operations  0.64 us (1%)
    pallas_call x1, Pallas kernels, per_device(): pl.pallas_call(functools.partial(kernel, ring, side, slots), out_shape=(p...  52.9 us
    unnamed x2, local copies, waits for them, and re-layouts  1.34 us

profile of v6, /device:TPU:1, one launch (start us, length us, event | category | flops | bytes accessed | tf_op | source)
XLA Modules:
  0.0 54.8 jit_solution(7264958206323379639)
XLA Ops:
  0.6 52.9 %shard_map.50 = (f32[4,112,128]{2,1,0:T(8,128)S(1)}, bf16[4,112,128]{2,1,0:T(8,128)(2,1)S(1)}) custom-call(bf16[1,64,112,128]{3,2,1,0:T(8,128)(2,1)} %grad.1, f32[4,112,128]{2,1,0:T(8,128)} %momentum.1, s32[64]{0:T(128)} %row_counts.1), custom_call_target="tpu_custom_call" | custom-call | tf_op jit(solution)/shard_map/pallas_call | solution.py:339
  53.5 0.7 %copy.7 = f32[4,112,128]{2,1,0:T(8,128)} copy(f32[4,112,128]{2,1,0:T(8,128)S(1)} %get-tuple-element.2) | data formatting | bytes 458752
  54.2 0.6 %copy.8 = bf16[4,112,128]{2,1,0:T(8,128)(2,1)} copy(bf16[4,112,128]{2,1,0:T(8,128)(2,1)S(1)} %get-tuple-element.3) | data formatting | bytes 229376

commit v7 on v6

--- a/solution.py
+++ b/solution.py
@@ -286,8 +286,6 @@
         pack(a, finish_sum(2 * a), finish_sum(2 * a + 1))
         for d in far_first:
             to_owner(a, d).start()
-    for copy in list(exchange.values()) + list(hop.values()):
-        copy.wait_send()
     for a in reversed(pairs):
         value = packed[a, place(a)]
         for d in reversed(far_first):
@@ -315,6 +313,8 @@
         for d in reversed(far_first):
             to_user(a, d).wait_recv()
 
+    for copy in list(exchange.values()) + list(hop.values()):
+        copy.wait_send()
     values = iterate([rounded[j] for j in range(mats)], unpack(0) + unpack(1), eye)
     for j, value in enumerate(values):
         count = jnp.full((1, 1), counts[replica * mats + j], jnp.int32)

time: 55.3 us -> 55.3 us (level)
  no operation moved by 1% of the time
where the time goes in v7:
time: 55.3 us; the launch traced here: 54.9 us
  Pallas kernels  52.9 us (96%)
  local copies, waits for them, and re-layouts  1.34 us (2%)
  between operations  0.64 us (1%)
    pallas_call x1, Pallas kernels, per_device(): pl.pallas_call(functools.partial(kernel, ring, side, slots), out_shape=(p...  52.9 us
    unnamed x2, local copies, waits for them, and re-layouts  1.34 us

profile of v7, /device:TPU:1, one launch (start us, length us, event | category | flops | bytes accessed | tf_op | source)
XLA Modules:
  0.0 54.9 jit_solution(12204018723324947410)
XLA Ops:
  0.6 52.9 %shard_map.50 = (f32[4,112,128]{2,1,0:T(8,128)S(1)}, bf16[4,112,128]{2,1,0:T(8,128)(2,1)S(1)}) custom-call(bf16[1,64,112,128]{3,2,1,0:T(8,128)(2,1)} %grad.1, f32[4,112,128]{2,1,0:T(8,128)} %momentum.1, s32[64]{0:T(128)} %row_counts.1), custom_call_target="tpu_custom_call" | custom-call | tf_op jit(solution)/shard_map/pallas_call | solution.py:339
  53.6 0.7 %copy.7 = f32[4,112,128]{2,1,0:T(8,128)} copy(f32[4,112,128]{2,1,0:T(8,128)S(1)} %get-tuple-element.2) | data formatting | bytes 458752
  54.3 0.6 %copy.8 = bf16[4,112,128]{2,1,0:T(8,128)(2,1)} copy(bf16[4,112,128]{2,1,0:T(8,128)(2,1)S(1)} %get-tuple-element.3) | data formatting | bytes 229376
